TPU v7x, 128 devices: a whole 4x4x4 slice. The times are simulated.
128 devices in a mesh: seq: 32 (over z, y, core), fsdp: 4 (over x).
Axes of the slice: x: 4, y: 4, z: 4, core: 2. Of those that a mesh axis runs over, the one named last changes fastest.
Arguments:
- self_query: bfloat16 [4, 8192, 2048], P('fsdp', 'seq'), may hold values from -8 to 8, as said below
- self_key: bfloat16 [4, 8192, 2048], P('fsdp', 'seq'), may hold values from -8 to 8, as said below
- self_value: bfloat16 [4, 8192, 2048], P('fsdp', 'seq'), may hold values from -6 to 6
- cross_query: bfloat16 [4, 8192, 2048], P('fsdp', 'seq'), may hold values from -6 to 6
- neighbours: bfloat16 [4, 128, 256, 768], P('fsdp', 'seq'), may hold values from -6 to 6
- neighbour_count: int32 [4, 128], P('fsdp', 'seq'), may hold values from 1 to 2
- kv_weight: bfloat16 [768, 4096], P('fsdp'), may hold values from -0.21875 to 0.21875
- out_grad: bfloat16 [4, 8192, 2048], P('fsdp', 'seq'), may hold values from -6 to 6
Outputs:
- block_out: bfloat16 [4, 8192, 2048], P('fsdp', 'seq')
- query_grad: bfloat16 [4, 8192, 2048], P('fsdp', 'seq')
- key_grad: bfloat16 [4, 8192, 2048], P('fsdp', 'seq')
- value_grad: bfloat16 [4, 8192, 2048], P('fsdp', 'seq')
- cross_grad: bfloat16 [4, 8192, 2048], P('fsdp', 'seq')
- weight_grad: float32 [768, 4096], P(('seq', 'fsdp'))
Inputs may be any that keep to these rules, and one draw needn't show every extreme that they name: `self_query`: entries of order one. `self_key`: entries of order one.
All inputs are finite; a program needn't handle non-finite values.
Results may differ from a plain program's by a relative error of at most 0.014.
Values may be sent and summed in bfloat16 or wider, within the bound.
A program may use at most 192 MiB of HBM per device.

v0:
```python
import jax
import jax.numpy as jnp
from jax import lax
from jax.sharding import PartitionSpec as P

HEADS = 16
HD = 128
GROUP = 64
RLEN = 128


neg_fill = -1e30


def from_behind(value, axis, steps):
    count = lax.axis_size(axis)
    first, last = (max(0, -steps), min(count, count - steps))
    return lax.ppermute(value, axis, [(source, source + steps) for source in range(first, last)])


def attend(queries, keys_in, values_in, grads, allowed, scaling):
    scores = (
        jnp.einsum("...qhd,...khd->...hqk", queries, keys_in, preferred_element_type=jnp.float32)
        * scaling
    )
    scores = jnp.where(allowed, scores, neg_fill)
    peaks = jnp.max(scores, axis=-1, keepdims=True)
    weights = jnp.exp(scores - peaks)
    probs = weights / jnp.sum(weights, axis=-1, keepdims=True)
    probs_low = probs.astype(jnp.bfloat16)
    output = jnp.einsum(
        "...hqk,...khd->...qhd", probs_low, values_in, preferred_element_type=jnp.float32
    )
    prob_grad = jnp.einsum(
        "...qhd,...khd->...hqk", grads, values_in, preferred_element_type=jnp.float32
    )
    row_delta = jnp.sum(probs * prob_grad, axis=-1, keepdims=True)
    score_grad = (probs * (prob_grad - row_delta) * scaling).astype(jnp.bfloat16)
    query_grad = jnp.einsum(
        "...hqk,...khd->...qhd", score_grad, keys_in, preferred_element_type=jnp.float32
    )
    key_grad = jnp.einsum(
        "...hqk,...qhd->...khd", score_grad, queries, preferred_element_type=jnp.float32
    )
    value_grad = jnp.einsum(
        "...hqk,...qhd->...khd", probs_low, grads, preferred_element_type=jnp.float32
    )
    return (output, query_grad, key_grad, value_grad)


def on_device(
    self_query, self_key, self_value, cross_query, neighbours, neighbour_count, kv_weight, out_grad
):
    tok_rows = self_query.shape[1]
    feature_width = self_query.shape[2]
    scaling = HD ** (-0.5)
    is_first = lax.axis_index("seq") == 0

    def head_view(array):
        return array.reshape(array.shape[:-1] + (HEADS, HD))

    prev_key, prev_value = from_behind((self_key, self_value), "seq", 1)
    all_keys = jnp.concatenate([prev_key[0], self_key[0]], 0)
    all_values = jnp.concatenate([prev_value[0], self_value[0]], 0)
    row_index = jnp.arange(tok_rows, dtype=jnp.int32)[:, None]
    col_index = jnp.arange(2 * tok_rows, dtype=jnp.int32)[None, :]
    self_allowed = (
        (col_index > row_index)
        & (col_index <= row_index + tok_rows)
        & ((col_index >= tok_rows) | jnp.logical_not(is_first))
    )
    self_out, self_qgrad, self_kterms, self_vterms = attend(
        head_view(self_query[0]),
        head_view(all_keys),
        head_view(all_values),
        head_view(out_grad[0]),
        self_allowed[None],
        scaling,
    )
    self_kterms = self_kterms.reshape(2 * tok_rows, feature_width)
    self_vterms = self_vterms.reshape(2 * tok_rows, feature_width)
    returned_key, returned_value = (
        from_behind(self_kterms[:tok_rows].astype(jnp.bfloat16), "seq", -1).astype(jnp.float32),
        from_behind(self_vterms[:tok_rows].astype(jnp.bfloat16), "seq", -1).astype(jnp.float32),
    )
    key_grad = (self_kterms[tok_rows:] + returned_key).astype(jnp.bfloat16)
    value_grad = (self_vterms[tok_rows:] + returned_value).astype(jnp.bfloat16)
    groups = tok_rows // GROUP
    encodings = neighbours[0]
    neigh_rows = encodings.shape[1]
    enc_width = encodings.shape[2]
    counts = neighbour_count[0].astype(jnp.bfloat16)
    rows_in = encodings.reshape(groups * neigh_rows, enc_width)
    columns = rows_in
    own_proj = (
        jnp.dot(
            columns,
            lax.all_gather(kv_weight, "fsdp", axis=0, tiled=True),
            preferred_element_type=jnp.float32,
        )
        .astype(jnp.bfloat16)
        .reshape(groups, neigh_rows, 2 * feature_width)
    )
    last_proj, last_count = from_behind((own_proj[groups - 1], counts[groups - 1 :]), "seq", 1)
    kv_proj = jnp.concatenate([last_proj[None], own_proj[: groups - 1]], 0)
    used_count = jnp.concatenate([last_count, counts[: groups - 1]], 0).astype(jnp.float32)
    neighbour_of = (jnp.arange(neigh_rows, dtype=jnp.int32) // RLEN).astype(jnp.float32)
    cross_allowed = (neighbour_of[None, :] < used_count[:, None])[:, None, None, :]
    group_keys = kv_proj[..., :feature_width].reshape(groups, neigh_rows, HEADS, HD)
    group_values = kv_proj[..., feature_width:].reshape(groups, neigh_rows, HEADS, HD)
    group_view = (groups, GROUP, HEADS, HD)
    cross_out, cross_qgrad, cross_kgrad, cross_vgrad = attend(
        cross_query[0].reshape(group_view),
        group_keys,
        group_values,
        out_grad[0].reshape(group_view),
        cross_allowed,
        scaling,
    )
    group_live = (jnp.arange(groups, dtype=jnp.int32) > 0) | jnp.logical_not(is_first)
    live_rows = group_live[:, None, None, None]
    cross_out = jnp.where(live_rows, cross_out, 0.0)
    cross_qgrad = jnp.where(live_rows, cross_qgrad, 0.0)
    kv_grad = jnp.concatenate(
        [
            cross_kgrad.reshape(groups, neigh_rows, feature_width),
            cross_vgrad.reshape(groups, neigh_rows, feature_width),
        ],
        -1,
    )
    kv_grad = jnp.where(group_live[:, None, None], kv_grad, 0.0).astype(jnp.bfloat16)
    returned_kv = from_behind(kv_grad[0], "seq", -1)
    grad_rows = encodings.reshape(groups * neigh_rows, enc_width)
    grad_kv = jnp.concatenate([kv_grad[1:], returned_kv[None]], 0).reshape(
        groups * neigh_rows, 2 * feature_width
    )
    columns = grad_rows
    weight_grad = lax.psum_scatter(
        jnp.einsum("re,rc->ec", columns, grad_kv, preferred_element_type=jnp.float32),
        ("seq", "fsdp"),
        scatter_dimension=0,
        tiled=True,
    )
    block_out = (
        self_out.reshape(tok_rows, feature_width) + cross_out.reshape(tok_rows, feature_width)
    ).astype(jnp.bfloat16)
    query_grad = self_qgrad.reshape(tok_rows, feature_width).astype(jnp.bfloat16)
    cross_grad = cross_qgrad.reshape(tok_rows, feature_width).astype(jnp.bfloat16)
    return (
        block_out[None],
        query_grad[None],
        key_grad[None],
        value_grad[None],
        cross_grad[None],
        weight_grad,
    )


def solution(mesh):
    in_specs = (
        P("fsdp", "seq", None),
        P("fsdp", "seq", None),
        P("fsdp", "seq", None),
        P("fsdp", "seq", None),
        P("fsdp", "seq", None, None),
        P("fsdp", "seq"),
        P("fsdp", None),
        P("fsdp", "seq", None),
    )
    out_specs = (
        P("fsdp", "seq", None),
        P("fsdp", "seq", None),
        P("fsdp", "seq", None),
        P("fsdp", "seq", None),
        P("fsdp", "seq", None),
        P(("seq", "fsdp"), None),
    )
    return jax.shard_map(
        on_device, mesh=mesh, in_specs=in_specs, out_specs=out_specs, check_vma=False
    )
```

profile of v0, /device:TPU:0, one launch (start us, length us, event | category | flops | bytes accessed | tf_op | source)
XLA Modules:
  0.0 451.3 jit_solution(12350276214869502606)
XLA Ops:
  8.0 69.9 %all-gather.2.cloned.1.call-done = bf16[768,4096]{1,0:T(8,128)(2,1)} async-done(((bf16[192,4096]{1,0:T(8,128)(2,1)}), bf16[768,4096]{1,0:T(8,128)(2,1)}) %all-gather.2.cloned.1.call-update) | async-done | bytes 6291472 | tf_op jit(solution)/shard_map/all_gather | solution.py:98
  77.8 9.9 %convolution_convert_fusion = bf16[1024,4096]{1,0:T(8,128)(2,1)S(1)} fusion(bf16[1024,768]{1,0:T(8,128)(2,1)S(1)} %bitcast.154, bf16[768,4096]{1,0:T(8,128)(2,1)} %all-gather.2.cloned.1.call-done), kind=kOutput, calls=%fused_computation.17 | convolution fusion | flops 6446645248 | bytes 16252928 | tf_op jit(solution)/shard_map/dot_general | solution.py:96
  87.8 3.2 copy-done.6
  91.0 1.6 slice.73
  92.5 3.0 collective-permute-start.2
  96.1 2.9 collective-permute-start.3
  99.1 1.3 copy.76
  100.4 2.8 collective-permute-start.1
  103.2 1.5 copy.125
  104.7 2.4 copy.126
  107.9 6.3 %slice.74 = bf16[768,4096]{1,0:T(8,128)(2,1)} slice(bf16[1024,4096]{1,0:T(8,128)(2,1)} %copy-done.6), slice={[0:768], [0:4096]} | slice | bytes 12582912 | tf_op jit(solution)/shard_map/slice | solution.py:105
  114.2 8.6 %copy.83 = bf16[3,256,4096]{1,2,0:T(8,128)(2,1)} copy(bf16[3,256,4096]{2,1,0:T(8,128)(2,1)} %bitcast.158) | data formatting | bytes 12582912 | tf_op jit(solution)/shard_map/slice | solution.py:105
  122.8 4.1 copy.82
  126.9 4.0 pad_maximum_fusion.1
  131.0 3.1 fusion.43
  136.1 1.8 fusion.69
  138.0 1.9 copy-done.18
  139.9 3.2 fusion.39
  143.0 30.6 %fusion.31 = bf16[4,16,256,128]{2,3,1,0:T(8,128)(2,1)} fusion(f32[4,16,256,64]{2,3,1,0:T(8,128)} %fusion.43, bf16[4,64,16,128]{3,2,1,0:T(8,128)(2,1)S(1)} %bitcast.167, f32[4,16,64,256]{3,2,1,0:T(8,128)} %copy-done.18, f32[4,16,64]{2,1,0:T(8,128)S(1)} %get-tuple-element.28), kind=kOutput, calls=%fused_computation.58 | convolution fusion | flops 275779840 | bytes 13647872 | tf_op jit(solution)/shard_map/...hqk,...qhd->...khd/dot_general | solution.py:42
  173.6 6.3 %copy.108 = bf16[4,256,2048]{2,1,0:T(8,128)(2,1)} copy(bf16[4,256,2048]{1,2,0:T(8,128)(2,1)} %bitcast.170) | data formatting | bytes 8388608 | tf_op jit(solution)/shard_map/reshape | solution.py:127
  179.9 6.3 %copy.107 = bf16[4,256,2048]{2,1,0:T(8,128)(2,1)} copy(bf16[4,256,2048]{1,2,0:T(8,128)(2,1)} %bitcast.171) | data formatting | bytes 8388608 | tf_op jit(solution)/shard_map/reshape | solution.py:126
  186.2 5.0 %fusion.4 = bf16[4,256,4096]{2,1,0:T(8,128)(2,1)S(1)} fusion(bf16[4,256,2048]{2,1,0:T(8,128)(2,1)} %copy.108, bf16[4,256,2048]{2,1,0:T(8,128)(2,1)} %copy.107, pred[4]{0:T(512)(128)(4,1)S(1)} %compare_or_fusion), kind=kLoop, calls=%fused_computation.5 | loop fusion | flops 20971520 | bytes 16777220 | tf_op jit(solution)/shard_map/convert_element_type | solution.py:131
  191.2 3.2 copy-done.2
  194.4 1.6 slice_bitcast_fusion
  196.0 1.3 collective-permute-start.6
  197.3 15.8 %collective-permute-start = (bf16[1,256,2048]{2,1,0:T(8,128)(2,1)}, bf16[1,256,2048]{2,1,0:T(8,128)(2,1)}, u32[]{:S(2)}, u32[]{:S(2)}) collective-permute-start(bf16[1,256,2048]{2,1,0:T(8,128)(2,1)} %param.10), channel_id=1, source_target_pairs={{0,4},{4,8},{8,12},{12,16},{16,20},{20,24},{24,28},{28,32},{32,36}... | collective-permute-start | bytes 3145736 | tf_op jit(solution)/shard_map/ppermute | solution.py:18
  213.1 2.3 copy.75
  215.4 1.3 copy.124
  216.7 1.6 copy.79
  218.3 2.3 copy.123
  221.4 2.3 copy.78
  223.7 2.9 fusion.34
  226.6 5.6 %fusion.68 = (f32[16,256]{1,0:T(8,128)S(1)}, f32[16,256,512]{1,2,0:T(8,128)}) fusion(f32[16,512,256]{2,1,0:T(8,128)S(1)} %fusion.34, pred[256,512]{0,1:T(8,128)(4,1)S(1)} %copy-done.16), kind=kOutput, calls=%fused_computation.108 | output fusion | flops 12583423 | bytes 16924672 | tf_op jit(solution)/shard_map/sub | solution.py:28
  232.2 3.1 slice.81
  235.3 7.4 %pad_maximum_fusion = bf16[4,256,4096]{2,1,0:T(8,128)(2,1)} fusion(bf16[1,256,4096]{2,1,0:T(8,128)(2,1)} %bitcast.34, bf16[3,256,4096]{2,1,0:T(8,128)(2,1)} %slice.81), kind=kLoop, calls=%fused_computation.8 | loop fusion | flops 4194304 | bytes 16777216 | tf_op jit(solution)/shard_map/concatenate | solution.py:134
  242.6 12.9 %convolution_bitcast_fusion = f32[768,4096]{0,1:T(8,128)} fusion(bf16[1024,4096]{1,0:T(8,128)(2,1)} %bitcast.163, bf16[1024,768]{1,0:T(8,128)(2,1)S(1)} %bitcast.155), kind=kOutput, calls=%fused_computation.16 | convolution fusion | flops 6442450944 | bytes 22544384 | tf_op jit(solution)/shard_map/re,rc->ec/dot_general | solution.py:139
  256.7 4.9 %convolution_bitcast_fusion.1 = f32[512,16,128]{0,2,1:T(8,128)S(1)} fusion(bf16[256,16,128]{0,2,1:T(8,128)(2,1)S(1)} %bitcast.178, f32[16,256,512]{1,2,0:T(8,128)} %get-tuple-element.27, f32[16,256]{1,0:T(8,128)S(1)} %get-tuple-element.26), kind=kOutput, calls=%fused_computation.39 | convolution fusion | flops 541065216 | bytes 13647872 | tf_op jit(solution)/shard_map/...hqk,...qhd->...khd/dot_general | solution.py:45
  261.6 1.9 copy-done.12
  263.7 1.4 copy.99
  265.1 2.3 copy.74
  267.4 6.9 %fusion.35 = f32[16,512,256]{2,1,0:T(8,128)} fusion(bf16[256,16,128]{0,2,1:T(8,128)(2,1)} %bitcast.177, bf16[256,16,128]{0,2,1:T(8,128)(2,1)} %bitcast.175, bf16[256,16,128]{0,2,1:T(8,128)(2,1)} %bitcast.181), kind=kOutput, calls=%fused_computation.62 | convolution fusion | flops 541065216 | bytes 11534336 | tf_op jit(solution)/shard_map/...qhd,...khd->...hqk/dot_general | solution.py:34
  274.3 15.0 %fusion.23 = f32[512,16,128]{0,2,1:T(8,128)} fusion(bf16[256,16,128]{0,2,1:T(8,128)(2,1)S(1)} %bitcast.180, f32[16,512,256]{2,1,0:T(8,128)} %fusion.35, f32[16,256,512]{1,2,0:T(8,128)} %get-tuple-element.27, f32[16,256]{1,0:T(8,128)S(1)} %get-tuple-element.26), kind=kOutput, calls=%fused_computation.38 | convolution fusion | flops 551555584 | bytes 22036480 | tf_op jit(solution)/shard_map/...hqk,...qhd->...khd/dot_general | solution.py:42
  289.3 1.8 slice.94
  291.1 1.4 copy.95
  292.6 1.5 collective-permute-start.4
  294.1 1.3 collective-permute-start.5
  295.4 6.7 %fusion.27 = f32[16,128,256]{2,1,0:T(8,128)} fusion(bf16[256,16,128]{0,2,1:T(8,128)(2,1)} %bitcast.176, bf16[256,16,128]{0,2,1:T(8,128)(2,1)} %bitcast.182, f32[16,256,512]{1,2,0:T(8,128)} %get-tuple-element.27, f32[16,256]{1,0:T(8,128)S(1)} %get-tuple-element.26), kind=kOutput, calls=%fused_computation.54 | convolution fusion | flops 545259520 | bytes 12599296 | tf_op jit(solution)/shard_map/...hqk,...khd->...qhd/dot_general | solution.py:31
  302.1 1.6 slice.79
  303.7 1.6 slice.77
  305.3 14.6 %fusion.33 = bf16[16,128,256]{2,1,0:T(8,128)(2,1)} fusion(f32[16,512,256]{2,1,0:T(8,128)} %fusion.35, bf16[256,16,128]{2,0,1:T(8,128)(2,1)S(1)} %copy.79, bf16[256,16,128]{2,0,1:T(8,128)(2,1)S(1)} %copy-done.9, f32[16,256,512]{1,2,0:T(8,128)} %get-tuple-element.27, f32[16,256]{1,0:T(8,128)S(1)} %get-tuple-element.26), kind=kOutput, calls=%fused_computation.60 | convolution fusion | flops 556274176 | bytes 19939328 | tf_op jit(solution)/shard_map/...hqk,...khd->...qhd/dot_general | solution.py:39
  319.9 2.3 copy.109
  322.2 3.0 copy.88
  325.1 2.9 copy.100
  328.0 2.9 copy.96
  330.9 3.3 fusion.37
  334.2 3.6 fusion.38
  337.8 1.8 select_bitcast_fusion
  339.7 2.6 copy.87
  342.2 2.7 reshape.232
  344.9 29.5 %fusion.36 = bf16[4,64,16,128]{3,1,2,0:T(8,128)(2,1)S(1)} fusion(bf16[4,256,16,128]{1,3,2,0:T(8,128)(2,1)} %bitcast.160, f32[4,16,256,64]{2,3,1,0:T(8,128)} %fusion.43, pred[4]{0:T(512)(128)(4,1)S(1)} %compare_or_fusion, f32[4,16,64,256]{3,2,1,0:T(8,128)} %copy-done.18, f32[4,16,64]{2,1,0:T(8,128)S(1)} %copy-done.21), kind=kOutput, calls=%fused_computation.63 | convolution fusion | flops 276828416 | bytes 13647876 | tf_op jit(solution)/shard_map/...hqk,...khd->...qhd/dot_general | solution.py:39
  376.4 3.6 add_convert_fusion.2
  380.0 57.3 %all-reduce.3.cloned.1.call-done = f32[768,4096]{0,1:T(8,128)} async-done(((f32[768,4096]{0,1:T(8,128)}), f32[768,4096]{0,1:T(8,128)}) %all-reduce.3.cloned.1.call-update) | async-done | bytes 12582928
  437.2 4.1 constant_dynamic-slice_fusion
  441.4 2.9 copy.110
  (70 shorter events, 8.4 us)
Async XLA Ops:
  7.2 70.7 %copy-start = (bf16[1,4,256,768]{3,2,1,0:T(8,128)(2,1)S(1)}, bf16[1,4,256,768]{3,2,1,0:T(8,128)(2,1)}, u32[]{:S(2)}) copy-start(bf16[1,4,256,768]{3,2,1,0:T(8,128)(2,1)} %param.12) | copy-start | bytes 4718596
  7.2 70.7 %all-gather.2.cloned.1.call-start = ((), (), s32[]{:S(2)}) async-start(), calls=%async_computation | async-start | bytes 7864320 | tf_op jit(solution)/shard_map/all_gather | solution.py:98
  7.9 429.3 %all-reduce.3.cloned.1.call-start = ((), (), s32[]{:S(2)}) async-start(), calls=%async_computation.1 | async-start | bytes 25165824
  87.8 3.2 copy-start.6
  91.0 4.6 %copy-start.17 = (s32[1,4]{1,0:T(1,128)S(1)}, s32[1,4]{1,0:T(1,128)}, u32[]{:S(2)}) copy-start(s32[1,4]{1,0:T(1,128)} %param.13) | copy-start | bytes 52
  91.0 8.1 %copy-start.15 = (bf16[1,256,2048]{2,1,0:T(8,128)(2,1)S(1)}, bf16[1,256,2048]{2,1,0:T(8,128)(2,1)}, u32[]{:S(2)}) copy-start(bf16[1,256,2048]{2,1,0:T(8,128)(2,1)} %param.9) | copy-start | bytes 3145732
  92.5 30.3 %collective-permute-start.2 = (bf16[256,4096]{1,0:T(8,128)(2,1)}, bf16[256,4096]{1,0:T(8,128)(2,1)}, u32[]{:S(2)}, u32[]{:S(2)}) collective-permute-start(bf16[256,4096]{1,0:T(8,128)(2,1)} %slice.73), channel_id=1, source_target_pairs={{0,4},{4,8},{8,12},{12,16},{16,20},{20,24},{24,28},{28,32},{32,36}... | collective-permute-start | bytes 6291464 | tf_op jit(solution)/shard_map/ppermute | solution.py:18
  96.1 11.0 %collective-permute-start.3 = (bf16[1]{0:T(256)(128)(2,1)}, bf16[1]{0:T(256)(128)(2,1)}, u32[]{:S(2)}, u32[]{:S(2)}) collective-permute-start(bf16[1]{0:T(256)(128)(2,1)} %bitcast.11), channel_id=1, source_target_pairs={{0,4},{4,8},{8,12},{12,16},{16,20},{20,24},{24,28},{28,32},{32,36}... | collective-permute-start | bytes 14 | tf_op jit(solution)/shard_map/ppermute | solution.py:18
  100.4 121.0 %collective-permute-start.1 = (bf16[1,256,2048]{1,2,0:T(8,128)(2,1)}, bf16[1,256,2048]{1,2,0:T(8,128)(2,1)}, u32[]{:S(2)}, u32[]{:S(2)}) collective-permute-start(bf16[1,256,2048]{1,2,0:T(8,128)(2,1)} %copy.76), channel_id=1, source_target_pairs={{0,4},{4,8},{8,12},{12,16},{16,20},{20,24},{24,28},{28,32},{32,36}... | collective-permute-start | bytes 3145736 | tf_op jit(solution)/shard_map/ppermute | solution.py:18
  126.9 4.0 copy-start.7
  131.0 3.2 copy-start.4
  131.0 4.5 copy-start.3
  137.9 1.9 copy-start.18
  137.9 5.1 %copy-start.20 = (f32[4,16,64]{2,1,0:T(8,128)}, f32[4,16,64]{2,1,0:T(8,128)S(1)}, u32[]{:S(2)}) copy-start(f32[4,16,64]{2,1,0:T(8,128)S(1)} %get-tuple-element.28) | copy-start | bytes 49156
  191.2 3.2 copy-start.2
  194.4 21.0 %copy-start.8 = (bf16[1,256,2048]{2,1,0:T(8,128)(2,1)S(1)}, bf16[1,256,2048]{2,1,0:T(8,128)(2,1)}, u32[]{:S(2)}) copy-start(bf16[1,256,2048]{2,1,0:T(8,128)(2,1)} %param.15) | copy-start | bytes 3145732
  196.0 39.3 %collective-permute-start.6 = (bf16[256,4096]{1,0:T(8,128)(2,1)}, bf16[256,4096]{1,0:T(8,128)(2,1)}, u32[]{:S(2)}, u32[]{:S(2)}) collective-permute-start(bf16[256,4096]{1,0:T(8,128)(2,1)} %slice_bitcast_fusion), channel_id=1, source_target_pairs={{4,0},{8,4},{12,8},{16,12},{20,16},{24,20},{28,24},{32,28},{36,32}... | collective-permute-start | bytes 6291464 | tf_op jit(solution)/shard_map/ppermute | solution.py:18
  197.3 67.8 %collective-permute-start = (bf16[1,256,2048]{2,1,0:T(8,128)(2,1)}, bf16[1,256,2048]{2,1,0:T(8,128)(2,1)}, u32[]{:S(2)}, u32[]{:S(2)}) collective-permute-start(bf16[1,256,2048]{2,1,0:T(8,128)(2,1)} %param.10), channel_id=1, source_target_pairs={{0,4},{4,8},{8,12},{12,16},{16,20},{20,24},{24,28},{28,32},{32,36}... | collective-permute-start | bytes 3145736 | tf_op jit(solution)/shard_map/ppermute | solution.py:18
  223.7 2.9 copy-start.16
  223.7 8.5 %slice-start = ((s8[8388608]{0:T(1024)(128)(4,1)}), s8[4194304]{0:T(1024)(128)(4,1)S(1)}, s32[]{:S(2)}) async-start(s8[8388608]{0:T(1024)(128)(4,1)} %bitcast.156), calls=%async_computation.2 | async-start | bytes 8388608
  226.6 5.6 %slice-start.1 = ((s8[8388608]{0:T(1024)(128)(4,1)}), s8[4194304]{0:T(1024)(128)(4,1)S(1)}, s32[]{:S(2)}) async-start(s8[8388608]{0:T(1024)(128)(4,1)} %bitcast.156), calls=%async_computation.3 | async-start | bytes 8388608
  255.5 1.2 copy-start.10
  261.6 1.9 copy-start.12
  267.4 6.9 %copy-start.11 = (bf16[1,256,2048]{1,2,0:T(8,128)(2,1)S(1)}, bf16[1,256,2048]{1,2,0:T(8,128)(2,1)}, u32[]{:S(2)}) copy-start(bf16[1,256,2048]{1,2,0:T(8,128)(2,1)} %copy.123) | copy-start | bytes 3145732
  292.5 9.5 %copy-start.13 = (f32[512,16,128]{0,2,1:T(8,128)S(1)}, f32[512,16,128]{0,2,1:T(8,128)}, u32[]{:S(2)}) copy-start(f32[512,16,128]{0,2,1:T(8,128)} %copy-done.12) | copy-start | bytes 12582916
  292.6 38.4 %collective-permute-start.4 = (bf16[256,2048]{1,0:T(8,128)(2,1)}, bf16[256,2048]{1,0:T(8,128)(2,1)}, u32[]{:S(2)}, u32[]{:S(2)}) collective-permute-start(bf16[256,2048]{1,0:T(8,128)(2,1)} %copy.95), channel_id=1, source_target_pairs={{4,0},{8,4},{12,8},{16,12},{20,16},{24,20},{28,24},{32,28},{36,32}... | collective-permute-start | bytes 3145736 | tf_op jit(solution)/shard_map/ppermute | solution.py:18
  294.1 40.1 %collective-permute-start.5 = (bf16[256,2048]{1,0:T(8,128)(2,1)}, bf16[256,2048]{1,0:T(8,128)(2,1)}, u32[]{:S(2)}, u32[]{:S(2)}) collective-permute-start(bf16[256,2048]{1,0:T(8,128)(2,1)} %copy.99), channel_id=1, source_target_pairs={{4,0},{8,4},{12,8},{16,12},{20,16},{24,20},{28,24},{32,28},{36,32}... | collective-permute-start | bytes 3145736 | tf_op jit(solution)/shard_map/ppermute | solution.py:18
  295.4 8.3 %copy-start.14 = (f32[512,16,128]{0,2,1:T(8,128)S(1)}, f32[512,16,128]{0,2,1:T(8,128)}, u32[]{:S(2)}) copy-start(f32[512,16,128]{0,2,1:T(8,128)} %fusion.23) | copy-start | bytes 12582916
  302.1 3.2 copy-start.9
  328.0 9.8 %copy-start.21 = (f32[4,16,64]{2,1,0:T(8,128)S(1)}, f32[4,16,64]{2,1,0:T(8,128)}, u32[]{:S(2)}) copy-start(f32[4,16,64]{2,1,0:T(8,128)} %copy-done.20) | copy-start | bytes 49156
  330.9 6.9 %copy-start.5 = (bf16[4,256,2048]{1,2,0:T(8,128)(2,1)S(1)}, bf16[4,256,2048]{1,2,0:T(8,128)(2,1)}, u32[]{:S(2)}) copy-start(bf16[4,256,2048]{1,2,0:T(8,128)(2,1)} %copy-done.4) | copy-start | bytes 12582916
  330.9 6.9 %copy-start.19 = (f32[4,16,64,256]{3,2,1,0:T(8,128)S(1)}, f32[4,16,64,256]{3,2,1,0:T(8,128)}, u32[]{:S(2)}) copy-start(f32[4,16,64,256]{3,2,1,0:T(8,128)} %copy-done.18) | copy-start | bytes 12582916
  376.4 67.8 %copy-start.1 = (bf16[1,4,256,768]{3,2,1,0:T(8,128)(2,1)S(1)}, bf16[1,4,256,768]{3,2,1,0:T(8,128)(2,1)}, u32[]{:S(2)}) copy-start(bf16[1,4,256,768]{3,2,1,0:T(8,128)(2,1)} %param.12) | copy-start | bytes 4718596
Sparse Core Ops, SparseCore 0:
  9.7 68.1 all-gather.1
  255.7 181.5 all-reduce.2
where the time goes:
time: 456 us; the launch traced here: 451 us
  matrix products  143 us (31%)
  waiting for transfers between devices  128 us (28%)
  local copies, waits for them, and re-layouts  102 us (22%)
  other arithmetic  35.8 us (8%)
  starting transfers between devices  28.8 us (6%)
  between operations  14.6 us (3%)
    all_gather x1, waiting for transfers between devices, on_device(): lax.all_gather(kv_weight, 'fsdp', axis=0, tiled=True)  69.9 us
    unnamed x3, waiting for transfers between devices  58 us
    dot_general x2, matrix products, attend(): jnp.einsum('...hqk,...qhd->...khd', score_grad, queries, preferred_elemen...  45.6 us
    dot_general x2, matrix products, attend(): jnp.einsum('...hqk,...khd->...qhd', score_grad, keys_in, preferred_elemen...  44.1 us
    unnamed x55, local copies, waits for them, and re-layouts  29.5 us
    ppermute x7, starting transfers between devices, from_behind(): lax.ppermute(value, axis, [(source, source + steps) for source in range(f...  28.7 us
    slice x2, local copies, waits for them, and re-layouts, on_device(): kv_proj = jnp.concatenate([last_proj[None], own_proj[:groups - 1]], 0)  14.9 us
    dot_general x1, matrix products, on_device(): jnp.einsum('re,rc->ec', columns, grad_kv, preferred_element_type=jnp.floa...  12.9 us
  transfers between devices with their start and end apart: 9, of which 2 were waited for; matrix products, arithmetic and copies ran while one was open for 55% of the time, Pallas kernels for 0%

commit v1 on v0

v1 whole, which is shorter than its diff:
```python
import jax
import jax.numpy as jnp
import numpy as np
from jax import lax
from jax.experimental import pallas as pl
from jax.experimental.pallas import tpu as pltpu
from jax.sharding import PartitionSpec as P

HEADS = 16
HD = 128
GROUP = 64
RLEN = 128
ENC = 768
TOK = 256
PAIRS = 8
PW = 256
SLABS = 32
SCALE = HD**-0.5
MESH_ID = pl.DeviceIdType.MESH
F32 = jnp.float32
BF16 = jnp.bfloat16

NN = (((1,), (0,)), ((), ()))
NT = (((1,), (1,)), ((), ()))
TN = (((0,), (0,)), ((), ()))


def dot(a, b, dims=NN):
    return lax.dot_general(a, b, dims, preferred_element_type=F32)


def row_orders():
    sizes = {"z": 4, "y": 4, "c": 2, "x": 4}
    grids = np.meshgrid(*[np.arange(n) for n in (2, 4, 4, 4, 6)], indexing="ij")
    out = np.zeros((3, ENC, ENC), np.float32)
    for t, axes in enumerate(("xyz", "yzx", "zxy")):
        at = {"c": grids[0], axes[0]: grids[1], axes[1]: grids[2], axes[2]: grids[3]}
        natural = (((at["z"] * sizes["y"] + at["y"]) * 2 + at["c"]) * 4 + at["x"]) * 6 + grids[4]
        out[t, np.arange(ENC), natural.reshape(-1)] = 1.0
    return out.astype(BF16)


def mod(a, n):
    return lax.rem(a, n)


def kernel(
    q_h, k_h, v_h, cq_h, nb_h, cnt_s, w_h, do_h, pt_h,
    out_o, dq_o, dk_o, dv_o, dcq_o, dw_o,
    qv, cqv, dov, kv, nbx, ptv, nbt, wv, kvret, kvsend, kvown, stage,
    bias, selfout, dkv, cntv, cntsend,
    own, csend, crecv, own1, t1, s1send, s1recv, own2, s2send, s2recv, t2, s3buf, s3recv,
    load_sem, pt_sem, tok_sem, nb_sem, nbh_sem, cnt_sem, kvx_sem, w_sem, ret_sem, out_sem, rs_sem,
):
    s = lax.axis_index("seq")
    x = lax.axis_index("fsdp")
    c = mod(s, 2)
    y = mod(s // 2, 4)
    z = s // 8
    first = s == 0
    nxt = mod(s + 1, SLABS)
    prv = mod(s + SLABS - 1, SLABS)
    sib = s + 1 - 2 * c
    xr = mod(x + 1, 4)
    xl = mod(x + 3, 4)
    xa = mod(x + 2, 4)

    def seq_of(zz, yy):
        return (zz * 4 + yy) * 2 + c

    def dev(seq, fs):
        return {"seq": seq, "fsdp": fs}

    def remote(src, dst, ssem, rsem, where):
        return pltpu.make_async_remote_copy(
            src_ref=src, dst_ref=dst, send_sem=ssem, recv_sem=rsem, device_id=where, device_id_type=MESH_ID
        )

    def wait(ref, sem):
        pltpu.make_async_copy(ref, ref, sem).wait()

    def rows(start, size):
        return pl.ds(pl.multiple_of(start, 8), size)

    def cols(start, size):
        return pl.ds(pl.multiple_of(start, 128), size)

    def load_w(p, _):
        for half in range(2):
            pltpu.make_async_copy(
                w_h.at[:, cols(half * 2048 + p * PW, PW)],
                wv.at[p, rows(x * 192, 192), pl.ds(half * PW, PW)],
                load_sem.at[p],
            ).start()
        return 0

    lax.fori_loop(0, PAIRS, load_w, 0)
    own_nb = pltpu.make_async_copy(nb_h.at[pl.ds(0, 768)], nbx.at[pl.ds(256, 768)], nb_sem)
    own_nb.start()
    pt_copy = pltpu.make_async_copy(pt_h, ptv, pt_sem)
    pt_copy.start()

    def load_tokens(p, _):
        span = cols(p * PW, PW)
        for n, (src, dst) in enumerate(
            ((q_h, qv.at[p]), (do_h, dov.at[p]), (cq_h, cqv.at[p]), (k_h, kv.at[p, 0, pl.ds(256, 256)]), (v_h, kv.at[p, 1, pl.ds(256, 256)]))
        ):
            pltpu.make_async_copy(src.at[:, span], dst, tok_sem.at[p, n]).start()
        return 0

    lax.fori_loop(0, PAIRS, load_tokens, 0)

    for g in range(3):
        cntv[g + 1] = jnp.full((8, 128), cnt_s[0, g], jnp.int32)
    cntsend[...] = jnp.full((8, 128), cnt_s[0, 3], jnp.int32)
    s3buf[...] = jnp.zeros(s3buf.shape, F32)

    barrier = pltpu.get_barrier_semaphore()
    partners = [dev(sib, x), dev(nxt, x), dev(prv, x)]
    for d in range(1, 4):
        partners += [dev(s, mod(x + d, 4)), dev(seq_of(z, mod(y + d, 4)), x), dev(seq_of(mod(z + d, 4), y), x)]
    for partner in partners:
        pl.semaphore_signal(barrier, inc=1, device_id=partner, device_id_type=MESH_ID)
    pl.semaphore_wait(barrier, len(partners))

    def w_first(p):
        wait(wv.at[p, rows(x * 192, 192)], load_sem.at[p])
        piece = wv.at[p, rows(x * 192 + c * 96, 96)]
        for where in (xr, xl):
            remote(piece, piece, w_sem.at[0, p], w_sem.at[1, p], dev(s, where)).start()

    def w_second(p):
        wait(wv.at[p, pl.ds(0, 192)], w_sem.at[1, p])
        from_left = wv.at[p, rows(xl * 192 + c * 96, 48)]
        from_right = wv.at[p, rows(xr * 192 + c * 96 + 48, 48)]
        remote(from_left, from_left, w_sem.at[2, p], w_sem.at[3, p], dev(s, xr)).start()
        remote(from_right, from_right, w_sem.at[2, p], w_sem.at[3, p], dev(s, xl)).start()
        for shard in (xl, xr):
            piece = wv.at[p, rows(shard * 192 + c * 96, 96)]
            remote(piece, piece, w_sem.at[4, p], w_sem.at[5, p], dev(sib, x)).start()

    def w_third(p):
        wait(wv.at[p, pl.ds(0, 96)], w_sem.at[3, p])
        piece = wv.at[p, rows(xa * 192 + c * 96, 96)]
        remote(piece, piece, w_sem.at[4, p], w_sem.at[5, p], dev(sib, x)).start()

    def w_done(p):
        wait(wv.at[p, pl.ds(0, 288)], w_sem.at[5, p])

    w_first(0)
    halo = remote(nb_h.at[pl.ds(768, 256)], nbx.at[pl.ds(0, 256)], nbh_sem.at[0], nbh_sem.at[1], dev(nxt, x))
    halo.start()
    count_copy = remote(cntsend, cntv.at[0], cnt_sem.at[0], cnt_sem.at[1], dev(nxt, x))
    count_copy.start()

    def send_kv(p, _):
        span = cols(p * PW, PW)
        for n, src in enumerate((k_h, v_h)):
            remote(src.at[:, span], kv.at[p, n, pl.ds(0, 256)], kvx_sem.at[0, p], kvx_sem.at[1, p], dev(nxt, x)).start()
        return 0

    lax.fori_loop(0, PAIRS, send_kv, 0)
    w_first(1)
    w_first(2)

    key_at = lax.broadcasted_iota(jnp.int32, (512, TOK), 0)
    query_at = lax.broadcasted_iota(jnp.int32, (512, TOK), 1)
    allowed = (key_at > query_at) & (key_at <= query_at + TOK) & ((key_at >= TOK) | jnp.logical_not(first))
    bias[...] = jnp.where(allowed, 0.0, -1e30).astype(F32)

    pt_copy.wait()
    own_nb.wait()

    def reorder(n, _):
        t = n // 3
        g = mod(n, 3) + 1
        nbt[t, :, cols(g * 256, 256)] = dot(ptv[t], nbx[rows(g * 256, 256)], NT).astype(BF16)
        return 0

    lax.fori_loop(0, 9, reorder, 0)
    w_second(0)
    w_first(3)
    halo.wait_recv()

    def reorder_halo(t, _):
        nbt[t, :, pl.ds(0, 256)] = dot(ptv[t], nbx[pl.ds(0, 256)], NT).astype(BF16)
        return 0

    lax.fori_loop(0, 3, reorder_halo, 0)
    count_copy.wait_recv()
    w_third(0)
    w_second(1)

    def softmax_grads(sc, dp):
        e = jnp.exp(sc - jnp.max(sc, axis=0, keepdims=True))
        probs = e * (1.0 / jnp.sum(e, axis=0, keepdims=True))
        delta = jnp.sum(probs * dp, axis=0, keepdims=True)
        return probs, probs * (dp - delta) * SCALE

    def self_pair(p):
        for n, ref in enumerate((qv.at[p], dov.at[p], cqv.at[p], kv.at[p, 0, pl.ds(256, 256)], kv.at[p, 1, pl.ds(256, 256)])):
            wait(ref, tok_sem.at[p, n])
        wait(kv.at[p, :, pl.ds(0, 256)], kvx_sem.at[1, p])
        slot = mod(p, 3)
        for h in range(2):
            lanes = pl.ds(h * HD, HD)
            qh = qv[p, :, lanes]
            doh = dov[p, :, lanes]
            kh = kv[p, 0, :, lanes]
            vh = kv[p, 1, :, lanes]
            sc = dot(kh, qh, NT) * SCALE + bias[...]
            probs, ds = softmax_grads(sc, dot(vh, doh, NT))
            probs = probs.astype(BF16)
            ds = ds.astype(BF16)
            selfout[:, lanes] = dot(probs, vh, TN)
            stage[1, p, :, lanes] = dot(ds, kh, TN).astype(BF16)
            dk = dot(ds, qh)
            dv = dot(probs, doh)
            kvsend[p, 0, :, lanes] = dk[:TOK].astype(BF16)
            kvsend[p, 1, :, lanes] = dv[:TOK].astype(BF16)
            kvown[slot, 0, :, lanes] = dk[TOK:]
            kvown[slot, 1, :, lanes] = dv[TOK:]
        remote(kvsend.at[p], kvret.at[p], ret_sem.at[0, p], ret_sem.at[1, p], dev(prv, x)).start()

    def returned(p):
        wait(kvret.at[p], ret_sem.at[1, p])
        slot = mod(p, 3)
        for n, dst in enumerate((dk_o, dv_o)):
            stage[3 + n, p] = (kvown[slot, n] + kvret[p, n].astype(F32)).astype(BF16)
            pltpu.make_async_copy(stage.at[3 + n, p], dst.at[:, cols(p * PW, PW)], out_sem.at[3 + n, p]).start()

    def cross_pair(p):
        lane = lax.broadcasted_iota(jnp.int32, (GROUP, PW), 1)
        key_row = lax.broadcasted_iota(jnp.int32, (256, 128), 0)

        def one_group(g, _):
            tok = rows(g * GROUP, GROUP)
            proj = dot(nbx[rows(g * 256, 256)], wv[p]).astype(BF16)
            kp = proj[:, :PW]
            vp = proj[:, PW:]
            qg = cqv[p, tok, :]
            dog = dov[p, tok, :]
            zero = jnp.zeros((GROUP, PW), BF16)
            qb = jnp.concatenate([jnp.where(lane < HD, qg, zero), jnp.where(lane >= HD, qg, zero)], 0)
            dob = jnp.concatenate([jnp.where(lane < HD, dog, zero), jnp.where(lane >= HD, dog, zero)], 0)
            used = key_row < cntv[g, pl.ds(0, 1), :] * RLEN
            sc = jnp.where(used, dot(kp, qb, NT) * SCALE, -1e30)
            probs, ds = softmax_grads(sc, dot(vp, dob, NT))
            live = jnp.where(jnp.logical_and(first, g == 0), 0.0, 1.0).astype(F32)
            probs = (probs * live).astype(BF16)
            ds = (ds * live).astype(BF16)
            o = dot(probs, vp, TN)
            dq = dot(ds, kp, TN)
            o = jnp.concatenate([o[:GROUP, :HD], o[GROUP:, HD:]], 1)
            dq = jnp.concatenate([dq[:GROUP, :HD], dq[GROUP:, HD:]], 1)
            stage[0, p, tok, :] = (selfout[tok, :] + o).astype(BF16)
            stage[2, p, tok, :] = dq.astype(BF16)
            dkv[rows(g * 256, 256), pl.ds(0, PW)] = dot(ds, qb).astype(BF16)
            dkv[rows(g * 256, 256), pl.ds(PW, PW)] = dot(probs, dob).astype(BF16)
            return 0

        lax.fori_loop(0, 4, one_group, 0)
        for n, dst in enumerate((out_o, dq_o, dcq_o)):
            pltpu.make_async_copy(stage.at[n, p], dst.at[:, cols(p * PW, PW)], out_sem.at[n, p]).start()

    def places(u):
        t = mod(u, 3)
        i0, i1, i2 = (3 - t) // 3, mod(t, 2), t // 2
        return (i0, i1, i2), (i0 * x + i1 * y + i2 * z, i0 * y + i1 * z + i2 * x, i0 * z + i1 * x + i2 * y)

    def peer(u, order, d):
        (i0, i1, i2), _ = places(u)
        on = ((i0, i1, i2), (i2, i0, i1), (i1, i2, i0))[order]
        return dev(seq_of(mod(z + d * on[2], 4), mod(y + d * on[1], 4)), mod(x + d * on[0], 4))

    def weight_grad(p):
        slot = mod(p, 2)
        for n in range(2):
            u = 2 * p + n
            t = mod(u, 3)
            grads = dkv[:, pl.ds(n * PW, PW)]
            csend[u] = dot(nbt[t, rows((1 - c) * 384, 384), :], grads).astype(BF16)
            remote(csend.at[u], crecv.at[u], rs_sem.at[0, u], rs_sem.at[1, u], dev(sib, x)).start()
        for n in range(2):
            u = 2 * p + n
            t = mod(u, 3)
            grads = dkv[:, pl.ds(n * PW, PW)]
            own[slot, n] = dot(nbt[t, rows(c * 384, 384), :], grads)

    def rs_core(p, n):
        u = 2 * p + n
        slot = mod(p, 2)
        _, (m1, _, _) = places(u)
        wait(crecv.at[u], rs_sem.at[1, u])
        for d in (2, 1, 3):
            span = rows(mod(m1 + d, 4) * 96, 96)
            s1send[u, d - 1] = (own[slot, n, span, :] + crecv[u, span, :].astype(F32)).astype(BF16)
            remote(s1send.at[u, d - 1], s1recv.at[u, d - 1], rs_sem.at[2, u], rs_sem.at[3, u], peer(u, 0, d)).start()
        span = rows(m1 * 96, 96)
        own1[slot, n] = own[slot, n, span, :] + crecv[u, span, :].astype(F32)

    def rs_first(p, n):
        u = 2 * p + n
        slot = mod(p, 2)
        _, (_, m2, _) = places(u)
        wait(s1recv.at[u], rs_sem.at[3, u])
        t1[...] = own1[slot, n] + ((s1recv[u, 0].astype(F32) + s1recv[u, 1].astype(F32)) + s1recv[u, 2].astype(F32))
        for d in (2, 1, 3):
            s2send[u, d - 1] = t1[rows(mod(m2 + d, 4) * 24, 24), :]
            remote(s2send.at[u, d - 1], s2recv.at[u, d - 1], rs_sem.at[4, u], rs_sem.at[5, u], peer(u, 1, d)).start()
        own2[slot, n] = t1[rows(m2 * 24, 24), :]

    def rs_second(p, n):
        u = 2 * p + n
        slot = mod(p, 2)
        _, (_, _, m3) = places(u)
        wait(s2recv.at[u], rs_sem.at[5, u])
        total = own2[slot, n] + ((s2recv[u, 0] + s2recv[u, 1]) + s2recv[u, 2])
        for a in range(4):
            s3buf[u, a, pl.ds(0, 6), :] = total[a * 6 : a * 6 + 6]
        for d in (2, 1, 3):
            remote(s3buf.at[u, mod(m3 + d, 4)], s3recv.at[u, d - 1], rs_sem.at[6, u], rs_sem.at[7, u], peer(u, 2, d)).start()

    def rs_third(p, n):
        u = 2 * p + n
        _, (_, _, m3) = places(u)
        wait(s3recv.at[u], rs_sem.at[7, u])
        dw_o[:, cols(n * 2048 + p * PW, PW)] = s3buf[u, m3] + ((s3recv[u, 0] + s3recv[u, 1]) + s3recv[u, 2])

    def step(i, _):
        @pl.when(i < PAIRS - 2)
        def _():
            w_second(i + 2)

        @pl.when(i < PAIRS - 4)
        def _():
            w_first(i + 4)

        @pl.when(i < PAIRS)
        def _():
            self_pair(i)

        @pl.when(i < PAIRS - 1)
        def _():
            w_third(i + 1)

        for lag, stage_of in ((1, rs_core), (2, rs_first), (3, rs_second), (4, rs_third)):

            @pl.when((i >= lag) & (i < PAIRS + lag))
            def _(lag=lag, stage_of=stage_of):
                for n in range(2):
                    stage_of(i - lag, n)

        @pl.when((i >= 2) & (i < PAIRS + 2))
        def _():
            returned(i - 2)

        @pl.when(i < PAIRS)
        def _():
            w_done(i)
            cross_pair(i)
            weight_grad(i)

        return 0

    lax.fori_loop(0, PAIRS + 4, step, 0)

    halo.wait_send()
    count_copy.wait_send()

    def drain(p, _):
        wait(kv.at[p, :, pl.ds(0, 256)], kvx_sem.at[0, p])
        wait(wv.at[p, pl.ds(0, 192)], w_sem.at[0, p])
        wait(wv.at[p, pl.ds(0, 96)], w_sem.at[2, p])
        wait(wv.at[p, pl.ds(0, 288)], w_sem.at[4, p])
        wait(kvsend.at[p], ret_sem.at[0, p])
        for n, dst in enumerate((out_o, dq_o, dcq_o, dk_o, dv_o)):
            pltpu.make_async_copy(stage.at[n, p], dst.at[:, cols(p * PW, PW)], out_sem.at[n, p]).wait()
        for n in range(2):
            u = 2 * p + n
            wait(csend.at[u], rs_sem.at[0, u])
            wait(s1send.at[u], rs_sem.at[2, u])
            wait(s2send.at[u], rs_sem.at[4, u])
            wait(s3recv.at[u], rs_sem.at[6, u])
        return 0

    lax.fori_loop(0, PAIRS, drain, 0)


def on_device(
    self_query, self_key, self_value, cross_query, neighbours, neighbour_count, kv_weight, out_grad
):
    any_spec = pl.BlockSpec(memory_space=pl.ANY)
    slab = jax.ShapeDtypeStruct((TOK, HEADS * HD), BF16)
    dma = pltpu.SemaphoreType.DMA
    subs = 2 * PAIRS
    scratch = [
        pltpu.VMEM((PAIRS, TOK, PW), BF16),
        pltpu.VMEM((PAIRS, TOK, PW), BF16),
        pltpu.VMEM((PAIRS, TOK, PW), BF16),
        pltpu.VMEM((PAIRS, 2, 2 * TOK, PW), BF16),
        pltpu.VMEM((1024, ENC), BF16),
        pltpu.VMEM((3, ENC, ENC), BF16),
        pltpu.VMEM((3, ENC, 1024), BF16),
        pltpu.VMEM((PAIRS, ENC, 2 * PW), BF16),
        pltpu.VMEM((PAIRS, 2, TOK, PW), BF16),
        pltpu.VMEM((PAIRS, 2, TOK, PW), BF16),
        pltpu.VMEM((3, 2, TOK, PW), F32),
        pltpu.VMEM((5, PAIRS, TOK, PW), BF16),
        pltpu.VMEM((2 * TOK, TOK), F32),
        pltpu.VMEM((TOK, PW), F32),
        pltpu.VMEM((1024, 2 * PW), BF16),
        pltpu.VMEM((4, 8, 128), jnp.int32),
        pltpu.VMEM((8, 128), jnp.int32),
        pltpu.VMEM((2, 2, 384, PW), F32),
        pltpu.VMEM((subs, 384, PW), BF16),
        pltpu.VMEM((subs, 384, PW), BF16),
        pltpu.VMEM((2, 2, 96, PW), F32),
        pltpu.VMEM((96, PW), F32),
        pltpu.VMEM((subs, 3, 96, PW), BF16),
        pltpu.VMEM((subs, 3, 96, PW), BF16),
        pltpu.VMEM((2, 2, 24, PW), F32),
        pltpu.VMEM((subs, 3, 24, PW), F32),
        pltpu.VMEM((subs, 3, 24, PW), F32),
        pltpu.VMEM((24, PW), F32),
        pltpu.VMEM((subs, 4, 8, PW), F32),
        pltpu.VMEM((subs, 3, 8, PW), F32),
        dma((PAIRS,)),
        dma(()),
        dma((PAIRS, 5)),
        dma(()),
        dma((2,)),
        dma((2,)),
        dma((2, PAIRS)),
        dma((6, PAIRS)),
        dma((2, PAIRS)),
        dma((5, PAIRS)),
        dma((8, subs)),
    ]
    out, dq, dk, dv, dcq, dw = pl.pallas_call(
        kernel,
        out_shape=[slab] * 5 + [jax.ShapeDtypeStruct((8, 2 * HEADS * HD), F32)],
        in_specs=[any_spec] * 5 + [pl.BlockSpec(memory_space=pltpu.SMEM)] + [any_spec] * 3,
        out_specs=[any_spec] * 5 + [pl.BlockSpec(memory_space=pltpu.VMEM)],
        scratch_shapes=scratch,
        compiler_params=pltpu.CompilerParams(
            collective_id=0, has_side_effects=True, vmem_limit_bytes=60 * 1024 * 1024
        ),
        cost_estimate=pl.CostEstimate(flops=20_000_000_000, bytes_accessed=20_000_000, transcendentals=3_000_000),
    )(
        self_query[0],
        self_key[0],
        self_value[0],
        cross_query[0],
        neighbours.reshape(1024, ENC),
        neighbour_count,
        kv_weight,
        out_grad[0],
        jnp.asarray(row_orders()),
    )
    return out[None], dq[None], dk[None], dv[None], dcq[None], dw[:6]


def solution(mesh):
    in_specs = (
        P("fsdp", "seq", None),
        P("fsdp", "seq", None),
        P("fsdp", "seq", None),
        P("fsdp", "seq", None),
        P("fsdp", "seq", None, None),
        P("fsdp", "seq"),
        P("fsdp", None),
        P("fsdp", "seq", None),
    )
    out_specs = (
        P("fsdp", "seq", None),
        P("fsdp", "seq", None),
        P("fsdp", "seq", None),
        P("fsdp", "seq", None),
        P("fsdp", "seq", None),
        P(("seq", "fsdp"), None),
    )
    return jax.shard_map(
        on_device, mesh=mesh, in_specs=in_specs, out_specs=out_specs, check_vma=False
    )
```

time: 456 us -> 109 us (0.24)
  matrix products: 143 us -> 0 us
  waiting for transfers between devices: 128 us -> 0 us
  Pallas kernels: 0 us -> 98.8 us
  local copies, waits for them, and re-layouts: 102 us -> 8.88 us
  other arithmetic: 35.8 us -> 0 us
  starting transfers between devices: 28.8 us -> 0 us
  between operations: 14.6 us -> 0.66 us
    dot_general x14 -> x0, matrix products: 143 us -> none  [the longest x2 45.6 us: attend(): jnp.einsum('...hqk,...qhd->...khd', score_grad, queries, preferred_elemen...]
    pallas_call x0 -> x1, Pallas kernels: none -> 98.8 us  [on_device(): pl.pallas_call(kernel, out_shape=[slab] * 5 + [jax.ShapeDtypeStruct((8, 2...]
    all_gather x1 -> x0, waiting for transfers between devices: 69.9 us -> none  [on_device(): lax.all_gather(kv_weight, 'fsdp', axis=0, tiled=True)]
    unnamed x3 -> x0, waiting for transfers between devices: 58 us -> none
    slice x12 -> x0, local copies, waits for them, and re-layouts: 31.1 us -> none  [the longest x2 14.9 us: on_device(): kv_proj = jnp.concatenate([last_proj[None], own_proj[:groups - 1]], 0)]
    ppermute x7 -> x0, starting transfers between devices: 28.7 us -> none  [from_behind(): lax.ppermute(value, axis, [(source, source + steps) for source in range(f...]
    unnamed x55 -> x16, local copies, waits for them, and re-layouts: 29.5 us -> 8.88 us
    reshape x4 -> x0, local copies, waits for them, and re-layouts: 18.2 us -> none  [the longest x1 6.28 us: on_device(): cross_vgrad.reshape(groups, neigh_rows, feature_width)]
  transfers between devices with their start and end apart: 9 -> 0, of which waited for: 2 -> 0; matrix products, arithmetic and copies ran while one was open for 55% -> 0% of each run, Pallas kernels for 0% -> 0%
where the time goes in v1:
time: 109 us; the launch traced here: 108 us
  Pallas kernels  98.8 us (91%)
  local copies, waits for them, and re-layouts  8.88 us (8%)
    pallas_call x1, Pallas kernels, on_device(): pl.pallas_call(kernel, out_shape=[slab] * 5 + [jax.ShapeDtypeStruct((8, 2...  98.8 us
    unnamed x16, local copies, waits for them, and re-layouts  8.88 us

profile of v1, /device:TPU:0, one launch (start us, length us, event | category | flops | bytes accessed | tf_op | source)
XLA Modules:
  0.0 108.4 jit_solution(3015212304468847215)
XLA Ops:
  0.6 98.8 %shard_map.136 = (bf16[256,2048]{1,0:T(8,128)(2,1)}, bf16[256,2048]{1,0:T(8,128)(2,1)}, bf16[256,2048]{1,0:T(8,128)(2,1)}, bf16[256,2048]{1,0:T(8,128)(2,1)}, bf...) custom-call(bf16[256,2048]{1,0:T(8,128)(2,1)} %bitcast.19, bf16[256,2048]{1,0:T(8,128)(2,1)} %bitcast.20, ...), custom_call_target="tpu_custom_call" | custom-call | flops 20000000000 | bytes 20000000 | tf_op jit(solution)/shard_map/pallas_call | solution.py:440
  99.5 0.0 copy-start.3
  99.5 2.4 %copy.21 = bf16[1,256,2048]{2,1,0:T(8,128)(2,1)} copy(bf16[1,256,2048]{2,1,0:T(8,128)(2,1)} %bitcast.16) | data formatting | bytes 2097152
  101.9 0.0 copy-done.3
  101.9 0.0 copy-start.2
  101.9 1.0 copy.22
  102.8 0.6 copy-done.2
  103.5 0.0 copy-start.1
  103.5 1.0 copy.23
  104.4 0.6 copy-done.1
  105.1 0.0 copy-start
  105.1 1.0 copy.24
  106.0 0.6 copy-done
  106.7 0.0 copy-start.4
  106.7 1.0 copy.25
  107.6 0.1 copy-done.4
  107.7 0.7 copy.26
Async XLA Ops:
  99.5 2.4 %copy-start.3 = (bf16[256,2048]{1,0:T(8,128)(2,1)S(1)}, bf16[256,2048]{1,0:T(8,128)(2,1)}, u32[]{:S(2)}) copy-start(bf16[256,2048]{1,0:T(8,128)(2,1)} %get-tuple-element.13) | copy-start | bytes 3145732
  101.9 1.6 %copy-start.2 = (bf16[256,2048]{1,0:T(8,128)(2,1)S(1)}, bf16[256,2048]{1,0:T(8,128)(2,1)}, u32[]{:S(2)}) copy-start(bf16[256,2048]{1,0:T(8,128)(2,1)} %get-tuple-element.14) | copy-start | bytes 3145732
  103.5 1.6 %copy-start.1 = (bf16[256,2048]{1,0:T(8,128)(2,1)S(1)}, bf16[256,2048]{1,0:T(8,128)(2,1)}, u32[]{:S(2)}) copy-start(bf16[256,2048]{1,0:T(8,128)(2,1)} %get-tuple-element.15) | copy-start | bytes 3145732
  105.1 1.6 %copy-start = (bf16[256,2048]{1,0:T(8,128)(2,1)S(1)}, bf16[256,2048]{1,0:T(8,128)(2,1)}, u32[]{:S(2)}) copy-start(bf16[256,2048]{1,0:T(8,128)(2,1)} %get-tuple-element.16) | copy-start | bytes 3145732
  106.7 1.0 copy-start.4

commit v2 on v1

v2 whole, which is shorter than its diff:
```python
import jax
import jax.numpy as jnp
import numpy as np
from jax import lax
from jax.experimental import pallas as pl
from jax.experimental.pallas import tpu as pltpu
from jax.sharding import PartitionSpec as P

HEADS = 16
HD = 128
GROUP = 64
RLEN = 128
ENC = 768
TOK = 256
PAIRS = 8
PW = 256
SLABS = 32
SCALE = HD**-0.5
LOG2E = 1.4426950408889634
MESH_ID = pl.DeviceIdType.MESH
F32 = jnp.float32
BF16 = jnp.bfloat16

NN = (((1,), (0,)), ((), ()))
NT = (((1,), (1,)), ((), ()))
TN = (((0,), (0,)), ((), ()))


def dot(a, b, dims=NN):
    return lax.dot_general(a, b, dims, preferred_element_type=F32)


def row_orders():
    sizes = {"z": 4, "y": 4, "c": 2, "x": 4}
    grids = np.meshgrid(*[np.arange(n) for n in (2, 4, 4, 4, 6)], indexing="ij")
    out = np.zeros((3, ENC, ENC), np.float32)
    for t, axes in enumerate(("zyx", "yxz", "xzy")):
        at = {"c": grids[0], axes[0]: grids[1], axes[1]: grids[2], axes[2]: grids[3]}
        natural = (((at["z"] * sizes["y"] + at["y"]) * 2 + at["c"]) * 4 + at["x"]) * 6 + grids[4]
        out[t, np.arange(ENC), natural.reshape(-1)] = 1.0
    return out.astype(BF16)


def mod(a, n):
    return lax.rem(a, n)


def kernel(
    q_h, k_h, v_h, cq_h, nb_h, cnt_s, w_h, do_h, pt_h,
    out_o, dq_o, dk_o, dv_o, dcq_o, dw_o,
    qv, cqv, dov, kv, nbx, ptv, nbt, wv, kvret, kvsend, kvown, stage,
    bias, selfout, crossout, dkv, cntv, cntsend,
    own, csend, crecv, own1, t1, s1send, s1recv, own2, s2send, s2recv, own3, s3send, s3recv,
    load_sem, pt_sem, tok_sem, nb_sem, nbh_sem, cnt_sem, kvx_sem, w_sem, ret_sem, out_sem, rs_sem,
):
    s = lax.axis_index("seq")
    x = lax.axis_index("fsdp")
    c = mod(s, 2)
    y = mod(s // 2, 4)
    z = s // 8
    first = s == 0
    nxt = mod(s + 1, SLABS)
    prv = mod(s + SLABS - 1, SLABS)
    sib = s + 1 - 2 * c
    xr = mod(x + 1, 4)
    xl = mod(x + 3, 4)
    xa = mod(x + 2, 4)

    def seq_of(zz, yy):
        return (zz * 4 + yy) * 2 + c

    def dev(seq, fs):
        return {"seq": seq, "fsdp": fs}

    def remote(src, dst, ssem, rsem, where):
        return pltpu.make_async_remote_copy(
            src_ref=src, dst_ref=dst, send_sem=ssem, recv_sem=rsem, device_id=where, device_id_type=MESH_ID
        )

    def wait(ref, sem):
        pltpu.make_async_copy(ref, ref, sem).wait()

    def rows(start, size):
        return pl.ds(pl.multiple_of(start, 8), size)

    def cols(start, size):
        return pl.ds(pl.multiple_of(start, 128), size)

    barrier = pltpu.get_barrier_semaphore()
    partners = [dev(sib, x), dev(nxt, x), dev(prv, x)]
    for d in range(1, 4):
        partners += [dev(s, mod(x + d, 4)), dev(seq_of(z, mod(y + d, 4)), x), dev(seq_of(mod(z + d, 4), y), x)]
    for partner in partners:
        pl.semaphore_signal(barrier, inc=1, device_id=partner, device_id_type=MESH_ID)

    def load_w(p, _):
        for half in range(2):
            pltpu.make_async_copy(
                w_h.at[:, cols(half * 2048 + p * PW, PW)],
                wv.at[p, rows(x * 192, 192), pl.ds(half * PW, PW)],
                load_sem.at[p],
            ).start()
        return 0

    lax.fori_loop(0, PAIRS, load_w, 0)
    own_nb = pltpu.make_async_copy(nb_h.at[pl.ds(0, 768)], nbx.at[pl.ds(256, 768)], nb_sem)
    own_nb.start()
    pt_copy = pltpu.make_async_copy(pt_h, ptv, pt_sem)
    pt_copy.start()

    token_copies = [
        pltpu.make_async_copy(src, dst, tok_sem.at[n])
        for n, (src, dst) in enumerate(
            ((q_h, qv), (k_h, kv.at[0, pl.ds(256, 256)]), (v_h, kv.at[1, pl.ds(256, 256)]), (do_h, dov), (cq_h, cqv))
        )
    ]
    for copy in token_copies:
        copy.start()

    for g in range(3):
        cntv[g + 1] = jnp.full((8, 128), cnt_s[0, g], jnp.int32)
    cntsend[...] = jnp.full((8, 128), cnt_s[0, 3], jnp.int32)
    own3[...] = jnp.zeros(own3.shape, F32)

    pl.semaphore_wait(barrier, len(partners))

    def w_first(p):
        wait(wv.at[p, rows(x * 192, 192)], load_sem.at[p])
        piece = wv.at[p, rows(x * 192 + c * 96, 96)]
        for where in (xr, xl):
            remote(piece, piece, w_sem.at[0, p], w_sem.at[1, p], dev(s, where)).start()

    def w_second(p):
        wait(wv.at[p, pl.ds(0, 192)], w_sem.at[1, p])
        from_left = wv.at[p, rows(xl * 192 + c * 96, 48)]
        from_right = wv.at[p, rows(xr * 192 + c * 96 + 48, 48)]
        remote(from_left, from_left, w_sem.at[2, p], w_sem.at[3, p], dev(s, xr)).start()
        remote(from_right, from_right, w_sem.at[2, p], w_sem.at[3, p], dev(s, xl)).start()
        for shard in (xl, xr):
            piece = wv.at[p, rows(shard * 192 + c * 96, 96)]
            remote(piece, piece, w_sem.at[4, p], w_sem.at[5, p], dev(sib, x)).start()

    def w_third(p):
        wait(wv.at[p, pl.ds(0, 96)], w_sem.at[3, p])
        piece = wv.at[p, rows(xa * 192 + c * 96, 96)]
        remote(piece, piece, w_sem.at[4, p], w_sem.at[5, p], dev(sib, x)).start()

    def w_done(p):
        wait(wv.at[p, pl.ds(0, 288)], w_sem.at[5, p])

    w_first(0)
    halo = remote(nb_h.at[pl.ds(768, 256)], nbx.at[pl.ds(0, 256)], nbh_sem.at[0], nbh_sem.at[1], dev(nxt, x))
    halo.start()
    count_copy = remote(cntsend, cntv.at[0], cnt_sem.at[0], cnt_sem.at[1], dev(nxt, x))
    count_copy.start()

    def send_kv(p):
        span = cols(p * PW, PW)
        for n, src in enumerate((k_h, v_h)):
            remote(src.at[:, span], kv.at[n, pl.ds(0, 256), span], kvx_sem.at[0, p], kvx_sem.at[1, p], dev(nxt, x)).start()

    send_kv(0)
    w_first(1)
    send_kv(1)
    w_first(2)
    send_kv(2)

    key_at = lax.broadcasted_iota(jnp.int32, (384, 128), 0)
    query_at = lax.broadcasted_iota(jnp.int32, (384, 128), 1)
    for b in range(2):
        allowed = (key_at > query_at) & (key_at <= query_at + TOK)
        allowed = allowed & ((key_at + b * 128 >= TOK) | jnp.logical_not(first))
        bias[b] = jnp.where(allowed, 0.0, -1e30).astype(F32)

    pt_copy.wait()
    own_nb.wait()

    def reorder(n, _):
        t = n // 3
        g = mod(n, 3) + 1
        nbt[t, :, cols(g * 256, 256)] = dot(ptv[t], nbx[rows(g * 256, 256)], NT).astype(BF16)
        return 0

    lax.fori_loop(0, 9, reorder, 0)
    w_second(0)
    w_first(3)
    halo.wait_recv()

    def reorder_halo(t, _):
        nbt[t, :, pl.ds(0, 256)] = dot(ptv[t], nbx[pl.ds(0, 256)], NT).astype(BF16)
        return 0

    lax.fori_loop(0, 3, reorder_halo, 0)
    count_copy.wait_recv()
    w_third(0)
    w_second(1)
    for copy in token_copies:
        copy.wait()

    def softmax_grads(sc, dp):
        e = jnp.exp2(sc - jnp.max(sc, axis=0, keepdims=True))
        inv = 1.0 / jnp.sum(e, axis=0, keepdims=True)
        probs = e * inv
        delta = jnp.sum(e * dp, axis=0, keepdims=True) * inv
        return probs, probs * ((dp - delta) * SCALE)

    def self_pair(p):
        wait(kv.at[:, pl.ds(0, 256), cols(p * PW, PW)], kvx_sem.at[1, p])
        slot = mod(p, 4)
        zero = jnp.zeros((128, 128), BF16)
        for h in range(2):
            lanes = pl.ds(h * HD, HD)
            at = cols(p * PW + h * HD, HD)
            qh = qv[:, at]
            doh = dov[:, at]
            kh = kv[0, :, at]
            vh = kv[1, :, at]
            sc = dot(kh, qh, NT)
            dp = dot(vh, doh, NT)
            parts = []
            for b in range(2):
                near = slice(b * 128, b * 128 + 384)
                here = slice(b * 128, b * 128 + 128)
                probs, ds = softmax_grads(sc[near, here] * (SCALE * LOG2E) + bias[b], dp[near, here])
                parts.append((probs.astype(BF16), ds.astype(BF16)))
            for b, (probs, ds) in enumerate(parts):
                near = slice(b * 128, b * 128 + 384)
                selfout[p, pl.ds(b * 128, 128), lanes] = dot(probs, vh[near], TN)
                stage[1, pl.ds(b * 128, 128), at] = dot(ds, kh[near], TN).astype(BF16)

            def joined(n):
                return jnp.concatenate(
                    [jnp.concatenate([parts[0][n], zero], 0), jnp.concatenate([zero, parts[1][n]], 0)], 1
                )

            dv = dot(joined(0), doh)
            dk = dot(joined(1), qh)
            kvsend[p, 0, :, lanes] = dk[:TOK].astype(BF16)
            kvsend[p, 1, :, lanes] = dv[:TOK].astype(BF16)
            kvown[slot, 0, :, lanes] = dk[TOK:]
            kvown[slot, 1, :, lanes] = dv[TOK:]
        remote(kvsend.at[p], kvret.at[p], ret_sem.at[0, p], ret_sem.at[1, p], dev(prv, x)).start()
        write_out(1, dq_o, p)

    def write_out(n, dst, p):
        span = cols(p * PW, PW)
        pltpu.make_async_copy(stage.at[n, :, span], dst.at[:, span], out_sem.at[n, p]).start()

    def returned(p):
        wait(kvret.at[p], ret_sem.at[1, p])
        slot = mod(p, 4)
        for n, dst in enumerate((dk_o, dv_o)):
            stage[3 + n, :, cols(p * PW, PW)] = (kvown[slot, n] + kvret[p, n].astype(F32)).astype(BF16)
            write_out(3 + n, dst, p)

    def cross_pair(p):
        lane = lax.broadcasted_iota(jnp.int32, (GROUP, PW), 1)
        key_row = lax.broadcasted_iota(jnp.int32, (256, 128), 0)
        zero = jnp.zeros((GROUP, PW), BF16)
        span = cols(p * PW, PW)
        live = [jnp.where(first, 0.0, 1.0).astype(F32), None, None, None]

        def both(a):
            return jnp.concatenate([jnp.where(lane < HD, a, zero), jnp.where(lane >= HD, a, zero)], 0)

        def split(a):
            return jnp.concatenate([a[:GROUP, :HD], a[GROUP:, HD:]], 1)

        groups = range(4)
        toks = [pl.ds(g * GROUP, GROUP) for g in groups]
        proj = [dot(nbx[pl.ds(g * 256, 256)], wv[p]).astype(BF16) for g in groups]
        kp = [a[:, :PW] for a in proj]
        vp = [a[:, PW:] for a in proj]
        qb = [both(cqv[tok, span]) for tok in toks]
        dob = [both(dov[tok, span]) for tok in toks]
        sc = [dot(kp[g], qb[g], NT) for g in groups]
        dp = [dot(vp[g], dob[g], NT) for g in groups]
        low = []
        for g in groups:
            used = key_row < cntv[g, pl.ds(0, 1), :] * RLEN
            probs, ds = softmax_grads(jnp.where(used, sc[g] * (SCALE * LOG2E), -1e30), dp[g])
            if live[g] is not None:
                probs, ds = probs * live[g], ds * live[g]
            low.append((probs.astype(BF16), ds.astype(BF16)))
        for g, (probs, ds) in enumerate(low):
            dkv[pl.ds(g * 256, 256), pl.ds(0, PW)] = dot(ds, qb[g]).astype(BF16)
            dkv[pl.ds(g * 256, 256), pl.ds(PW, PW)] = dot(probs, dob[g]).astype(BF16)
        for g, (probs, ds) in enumerate(low):
            crossout[p, toks[g], :] = split(dot(probs, vp[g], TN))
            stage[2, toks[g], span] = split(dot(ds, kp[g], TN)).astype(BF16)
        write_out(2, dcq_o, p)

    def finish_out(p):
        span = cols(p * PW, PW)
        stage[0, :, span] = (selfout[p] + crossout[p]).astype(BF16)
        write_out(0, out_o, p)

    def kind(p, n):
        if n:
            return 1 + p // 4
        return mod(p, 4) // 2 * (1 - mod(p, 2)) * (2 - p // 4)

    def places(p, n):
        t = kind(p, n)
        a, b, e = (2 - t) // 2, mod(t, 2), t // 2
        return a * z + b * y + e * x, a * y + b * x + e * z, a * x + b * z + e * y

    def peer(p, n, order, d):
        t = kind(p, n)
        a, b, e = d * ((2 - t) // 2), d * mod(t, 2), d * (t // 2)
        dz, dy, dx = ((a, b, e), (e, a, b), (b, e, a))[order]
        return dev(seq_of(mod(z + dz, 4), mod(y + dy, 4)), mod(x + dx, 4))

    def weight_grad(p):
        slot = mod(p, 2)
        for n in range(2):
            u = 2 * p + n
            t = kind(p, n)
            grads = dkv[:, pl.ds(n * PW, PW)]
            csend[u] = dot(nbt[t, rows((1 - c) * 384, 384), :], grads).astype(BF16)
            remote(csend.at[u], crecv.at[u], rs_sem.at[0, u], rs_sem.at[1, u], dev(sib, x)).start()
        for n in range(2):
            u = 2 * p + n
            t = kind(p, n)
            grads = dkv[:, pl.ds(n * PW, PW)]
            own[slot, n] = dot(nbt[t, rows(c * 384, 384), :], grads)

    def rs_core(p, n):
        u = 2 * p + n
        slot = mod(p, 2)
        m1, _, _ = places(p, n)
        wait(crecv.at[u], rs_sem.at[1, u])
        for d in (2, 1, 3):
            span = rows(mod(m1 + d, 4) * 96, 96)
            s1send[u, d - 1] = (own[slot, n, span, :] + crecv[u, span, :].astype(F32)).astype(BF16)
            remote(s1send.at[u, d - 1], s1recv.at[u, d - 1], rs_sem.at[2, u], rs_sem.at[3, u], peer(p, n, 0, d)).start()
        span = rows(m1 * 96, 96)
        own1[p, n] = own[slot, n, span, :] + crecv[u, span, :].astype(F32)

    def rs_first(p, n):
        u = 2 * p + n
        slot = mod(p, 2)
        _, m2, _ = places(p, n)
        wait(s1recv.at[u], rs_sem.at[3, u])
        t1[...] = own1[p, n] + ((s1recv[u, 0].astype(F32) + s1recv[u, 1].astype(F32)) + s1recv[u, 2].astype(F32))
        for d in (2, 1, 3):
            piece = t1[rows(mod(m2 + d, 4) * 24, 24), :]
            s2send[u, d - 1] = jnp.concatenate([piece[:, :128], piece[:, 128:]], 0).astype(BF16)
            remote(s2send.at[u, d - 1], s2recv.at[u, d - 1], rs_sem.at[4, u], rs_sem.at[5, u], peer(p, n, 1, d)).start()
        own2[p, n] = t1[rows(m2 * 24, 24), :]

    def rs_second(p, n):
        u = 2 * p + n
        slot = mod(p, 2)
        _, _, m3 = places(p, n)
        wait(s2recv.at[u], rs_sem.at[5, u])
        got = [s2recv[u, d].astype(F32) for d in range(3)]
        got = (got[0] + got[1]) + got[2]
        total = own2[p, n] + jnp.concatenate([got[:24], got[24:]], 1)
        for a in range(4):
            piece = total[a * 6 : a * 6 + 6]
            own3[p, n, a, pl.ds(0, 6), :] = piece
            piece = jnp.concatenate([piece, jnp.zeros((2, PW), F32)], 0)
            s3send[u, a] = jnp.concatenate([piece[:, :128], piece[:, 128:]], 0).astype(BF16)
        for d in (2, 1, 3):
            remote(s3send.at[u, mod(m3 + d, 4)], s3recv.at[u, d - 1], rs_sem.at[6, u], rs_sem.at[7, u], peer(p, n, 2, d)).start()

    def rs_third(p, n):
        u = 2 * p + n
        _, _, m3 = places(p, n)
        wait(s3recv.at[u], rs_sem.at[7, u])
        got = [s3recv[u, d].astype(F32) for d in range(3)]
        got = (got[0] + got[1]) + got[2]
        dw_o[:, cols(n * 2048 + p * PW, PW)] = own3[p, n, m3] + jnp.concatenate([got[:8], got[8:]], 1)

    def step(i, _):
        @pl.when(i < PAIRS - 2)
        def _():
            w_second(i + 2)

        @pl.when(i < PAIRS - 3)
        def _():
            send_kv(i + 3)

        @pl.when(i < PAIRS - 4)
        def _():
            w_first(i + 4)

        @pl.when(i < PAIRS)
        def _():
            self_pair(i)

        @pl.when(i < PAIRS - 1)
        def _():
            w_third(i + 1)

        for lag, stage_of in ((1, rs_core), (3, rs_first), (5, rs_second), (7, rs_third)):

            @pl.when((i >= lag) & (i < PAIRS + lag))
            def _(lag=lag, stage_of=stage_of):
                for n in range(2):
                    stage_of(i - lag, n)

        @pl.when((i >= 3) & (i < PAIRS + 3))
        def _():
            returned(i - 3)

        @pl.when(i < PAIRS)
        def _():
            w_done(i)
            cross_pair(i)
            weight_grad(i)

            finish_out(i)

        return 0

    lax.fori_loop(0, PAIRS + 7, step, 0)

    halo.wait_send()
    count_copy.wait_send()

    def drain(p, _):
        wait(kv.at[:, pl.ds(0, 256), cols(p * PW, PW)], kvx_sem.at[0, p])
        wait(wv.at[p, pl.ds(0, 192)], w_sem.at[0, p])
        wait(wv.at[p, pl.ds(0, 96)], w_sem.at[2, p])
        wait(wv.at[p, pl.ds(0, 288)], w_sem.at[4, p])
        wait(kvsend.at[p], ret_sem.at[0, p])
        for n in range(5):
            wait(stage.at[n, :, cols(p * PW, PW)], out_sem.at[n, p])
        for n in range(2):
            u = 2 * p + n
            wait(csend.at[u], rs_sem.at[0, u])
            wait(s1send.at[u], rs_sem.at[2, u])
            wait(s2send.at[u], rs_sem.at[4, u])
            wait(s3recv.at[u], rs_sem.at[6, u])
        return 0

    lax.fori_loop(0, PAIRS, drain, 0)


def finish(*refs):
    ins, outs, slabs, tail, sem = refs[:6], refs[6:12], refs[12], refs[13], refs[14]
    held = [slabs.at[n] for n in range(5)] + [tail]
    reads = [pltpu.make_async_copy(a, b, sem.at[0, n]) for n, (a, b) in enumerate(zip(ins, held))]
    writes = [pltpu.make_async_copy(a, b, sem.at[1, n]) for n, (a, b) in enumerate(zip(held, outs))]
    for copy in reads:
        copy.start()
    for read, write in zip(reads, writes):
        read.wait()
        write.start()
    for copy in writes:
        copy.wait()


def on_device(
    self_query, self_key, self_value, cross_query, neighbours, neighbour_count, kv_weight, out_grad
):
    any_spec = pl.BlockSpec(memory_space=pl.ANY)
    slab = jax.ShapeDtypeStruct((TOK, HEADS * HD), BF16)
    dma = pltpu.SemaphoreType.DMA
    subs = 2 * PAIRS
    scratch = [
        pltpu.VMEM((TOK, HEADS * HD), BF16),
        pltpu.VMEM((TOK, HEADS * HD), BF16),
        pltpu.VMEM((TOK, HEADS * HD), BF16),
        pltpu.VMEM((2, 2 * TOK, HEADS * HD), BF16),
        pltpu.VMEM((1024, ENC), BF16),
        pltpu.VMEM((3, ENC, ENC), BF16),
        pltpu.VMEM((3, ENC, 1024), BF16),
        pltpu.VMEM((PAIRS, ENC, 2 * PW), BF16),
        pltpu.VMEM((PAIRS, 2, TOK, PW), BF16),
        pltpu.VMEM((PAIRS, 2, TOK, PW), BF16),
        pltpu.VMEM((4, 2, TOK, PW), F32),
        pltpu.VMEM((5, TOK, HEADS * HD), BF16),
        pltpu.VMEM((2, 384, 128), F32),
        pltpu.VMEM((PAIRS, TOK, PW), F32),
        pltpu.VMEM((PAIRS, TOK, PW), F32),
        pltpu.VMEM((1024, 2 * PW), BF16),
        pltpu.VMEM((4, 8, 128), jnp.int32),
        pltpu.VMEM((8, 128), jnp.int32),
        pltpu.VMEM((2, 2, 384, PW), F32),
        pltpu.VMEM((subs, 384, PW), BF16),
        pltpu.VMEM((subs, 384, PW), BF16),
        pltpu.VMEM((PAIRS, 2, 96, PW), F32),
        pltpu.VMEM((96, PW), F32),
        pltpu.VMEM((subs, 3, 96, PW), BF16),
        pltpu.VMEM((subs, 3, 96, PW), BF16),
        pltpu.VMEM((PAIRS, 2, 24, PW), F32),
        pltpu.VMEM((subs, 3, 48, 128), BF16),
        pltpu.VMEM((subs, 3, 48, 128), BF16),
        pltpu.VMEM((PAIRS, 2, 4, 8, PW), F32),
        pltpu.VMEM((subs, 4, 16, 128), BF16),
        pltpu.VMEM((subs, 3, 16, 128), BF16),
        dma((PAIRS,)),
        dma(()),
        dma((5,)),
        dma(()),
        dma((2,)),
        dma((2,)),
        dma((2, PAIRS)),
        dma((6, PAIRS)),
        dma((2, PAIRS)),
        dma((5, PAIRS)),
        dma((8, subs)),
    ]
    out, dq, dk, dv, dcq, dw = pl.pallas_call(
        kernel,
        out_shape=[slab] * 5 + [jax.ShapeDtypeStruct((8, 2 * HEADS * HD), F32)],
        in_specs=[any_spec] * 5 + [pl.BlockSpec(memory_space=pltpu.SMEM)] + [any_spec] * 3,
        out_specs=[any_spec] * 5 + [pl.BlockSpec(memory_space=pltpu.VMEM)],
        scratch_shapes=scratch,
        compiler_params=pltpu.CompilerParams(
            collective_id=0, has_side_effects=True, vmem_limit_bytes=60 * 1024 * 1024
        ),
        cost_estimate=pl.CostEstimate(flops=20_000_000_000, bytes_accessed=20_000_000, transcendentals=3_000_000),
    )(
        self_query[0],
        self_key[0],
        self_value[0],
        cross_query[0],
        neighbours.reshape(1024, ENC),
        neighbour_count,
        kv_weight,
        out_grad[0],
        jnp.asarray(row_orders()),
    )
    out, dq, dk, dv, dcq, dw = pl.pallas_call(
        finish,
        out_shape=[slab] * 5 + [jax.ShapeDtypeStruct((8, 2 * HEADS * HD), F32)],
        in_specs=[any_spec] * 6,
        out_specs=[any_spec] * 6,
        scratch_shapes=[
            pltpu.VMEM((5, TOK, HEADS * HD), BF16),
            pltpu.VMEM((8, 2 * HEADS * HD), F32),
            dma((2, 6)),
        ],
        cost_estimate=pl.CostEstimate(flops=0, bytes_accessed=10_000_000, transcendentals=0),
    )(out, dq, dk, dv, dcq, dw)
    return out[None], dq[None], dk[None], dv[None], dcq[None], dw[:6]


def solution(mesh):
    in_specs = (
        P("fsdp", "seq", None),
        P("fsdp", "seq", None),
        P("fsdp", "seq", None),
        P("fsdp", "seq", None),
        P("fsdp", "seq", None, None),
        P("fsdp", "seq"),
        P("fsdp", None),
        P("fsdp", "seq", None),
    )
    out_specs = (
        P("fsdp", "seq", None),
        P("fsdp", "seq", None),
        P("fsdp", "seq", None),
        P("fsdp", "seq", None),
        P("fsdp", "seq", None),
        P(("seq", "fsdp"), None),
    )
    return jax.shard_map(
        on_device, mesh=mesh, in_specs=in_specs, out_specs=out_specs, check_vma=False
    )
```

time: 109 us -> 82.7 us (0.76)
  Pallas kernels: 98.8 us -> 82 us
  local copies, waits for them, and re-layouts: 8.88 us -> 0 us
    pallas_call x1, Pallas kernels: 98.8 us -> 77.6 us  [on_device(): pl.pallas_call(kernel, out_shape=[slab] * 5 + [jax.ShapeDtypeStruct((8, 2...]
    unnamed x16 -> x0, local copies, waits for them, and re-layouts: 8.88 us -> none
    pallas_call x0 -> x1, Pallas kernels: none -> 4.43 us  [on_device(): pl.pallas_call(finish, out_shape=[slab] * 5 + [jax.ShapeDtypeStruct((8, 2...]
where the time goes in v2:
time: 82.7 us; the launch traced here: 82.6 us
  Pallas kernels  82 us (99%)
    pallas_call x1, Pallas kernels, on_device(): pl.pallas_call(kernel, out_shape=[slab] * 5 + [jax.ShapeDtypeStruct((8, 2...  77.6 us
    pallas_call x1, Pallas kernels, on_device(): pl.pallas_call(finish, out_shape=[slab] * 5 + [jax.ShapeDtypeStruct((8, 2...  4.43 us

profile of v2, /device:TPU:0, one launch (start us, length us, event | category | flops | bytes accessed | tf_op | source)
XLA Modules:
  0.0 82.6 jit_solution(2344486780011294859)
XLA Ops:
  0.6 77.6 %shard_map.136 = (bf16[256,2048]{1,0:T(8,128)(2,1)}, bf16[256,2048]{1,0:T(8,128)(2,1)}, bf16[256,2048]{1,0:T(8,128)(2,1)}, bf16[256,2048]{1,0:T(8,128)(2,1)}, bf...) custom-call(bf16[256,2048]{1,0:T(8,128)(2,1)} %bitcast.13, bf16[256,2048]{1,0:T(8,128)(2,1)} %bitcast.14, ...), custom_call_target="tpu_custom_call" | custom-call | flops 20000000000 | bytes 20000000 | tf_op jit(solution)/shard_map/pallas_call | solution.py:507
  78.2 4.4 %shard_map.137 = (bf16[256,2048]{1,0:T(8,128)(2,1)}, bf16[256,2048]{1,0:T(8,128)(2,1)}, bf16[256,2048]{1,0:T(8,128)(2,1)}, bf16[256,2048]{1,0:T(8,128)(2,1)}, bf...) custom-call(bf16[256,2048]{1,0:T(8,128)(2,1)} %get-tuple-element.18.refs_0_, bf16[256,2048]{1,0:T(8,128)(2,1)} %get-tuple-element.19.refs_1_, ...), custom_call_target="tpu_custom_call" | custom-call | bytes 10000000 | tf_op jit(solution)/shard_map/pallas_call | solution.py:528

commit v3 on v2

--- a/solution.py
+++ b/solution.py
@@ -206,7 +206,7 @@
 
     def self_pair(p):
         wait(kv.at[:, pl.ds(0, 256), cols(p * PW, PW)], kvx_sem.at[1, p])
-        slot = mod(p, 4)
+        slot = p
         zero = jnp.zeros((128, 128), BF16)
         for h in range(2):
             lanes = pl.ds(h * HD, HD)
@@ -248,7 +248,7 @@
 
     def returned(p):
         wait(kvret.at[p], ret_sem.at[1, p])
-        slot = mod(p, 4)
+        slot = p
         for n, dst in enumerate((dk_o, dv_o)):
             stage[3 + n, :, cols(p * PW, PW)] = (kvown[slot, n] + kvret[p, n].astype(F32)).astype(BF16)
             write_out(3 + n, dst, p)
@@ -386,12 +386,9 @@
         def _():
             w_first(i + 4)
 
-        @pl.when(i < PAIRS)
+        @pl.when(i < PAIRS - 1)
         def _():
             self_pair(i)
-
-        @pl.when(i < PAIRS - 1)
-        def _():
             w_third(i + 1)
 
         for lag, stage_of in ((1, rs_core), (3, rs_first), (5, rs_second), (7, rs_third)):
@@ -401,17 +398,20 @@
                 for n in range(2):
                     stage_of(i - lag, n)
 
-        @pl.when((i >= 3) & (i < PAIRS + 3))
-        def _():
-            returned(i - 3)
-
         @pl.when(i < PAIRS)
         def _():
             w_done(i)
             cross_pair(i)
             weight_grad(i)
 
-            finish_out(i)
+        @pl.when(i == PAIRS)
+        def _():
+            self_pair(PAIRS - 1)
+
+        @pl.when(i >= PAIRS - 1)
+        def _():
+            finish_out(i - PAIRS + 1)
+            returned(i - PAIRS + 1)
 
         return 0
 
@@ -471,7 +471,7 @@
         pltpu.VMEM((PAIRS, ENC, 2 * PW), BF16),
         pltpu.VMEM((PAIRS, 2, TOK, PW), BF16),
         pltpu.VMEM((PAIRS, 2, TOK, PW), BF16),
-        pltpu.VMEM((4, 2, TOK, PW), F32),
+        pltpu.VMEM((PAIRS, 2, TOK, PW), F32),
         pltpu.VMEM((5, TOK, HEADS * HD), BF16),
         pltpu.VMEM((2, 384, 128), F32),
         pltpu.VMEM((PAIRS, TOK, PW), F32),

time: 82.7 us -> 82.1 us (level)
  no operation moved by 1% of the time
where the time goes in v3:
time: 82.1 us; the launch traced here: 81.9 us
  Pallas kernels  81.3 us (99%)
    pallas_call x1, Pallas kernels, on_device(): pl.pallas_call(kernel, out_shape=[slab] * 5 + [jax.ShapeDtypeStruct((8, 2...  76.9 us
    pallas_call x1, Pallas kernels, on_device(): pl.pallas_call(finish, out_shape=[slab] * 5 + [jax.ShapeDtypeStruct((8, 2...  4.43 us

profile of v3, /device:TPU:0, one launch (start us, length us, event | category | flops | bytes accessed | tf_op | source)
XLA Modules:
  0.0 81.9 jit_solution(9093515480292541081)
XLA Ops:
  0.6 76.9 %shard_map.136 = (bf16[256,2048]{1,0:T(8,128)(2,1)}, bf16[256,2048]{1,0:T(8,128)(2,1)}, bf16[256,2048]{1,0:T(8,128)(2,1)}, bf16[256,2048]{1,0:T(8,128)(2,1)}, bf...) custom-call(bf16[256,2048]{1,0:T(8,128)(2,1)} %bitcast.13, bf16[256,2048]{1,0:T(8,128)(2,1)} %bitcast.14, ...), custom_call_target="tpu_custom_call" | custom-call | flops 20000000000 | bytes 20000000 | tf_op jit(solution)/shard_map/pallas_call | solution.py:507
  77.5 4.4 %shard_map.137 = (bf16[256,2048]{1,0:T(8,128)(2,1)}, bf16[256,2048]{1,0:T(8,128)(2,1)}, bf16[256,2048]{1,0:T(8,128)(2,1)}, bf16[256,2048]{1,0:T(8,128)(2,1)}, bf...) custom-call(bf16[256,2048]{1,0:T(8,128)(2,1)} %get-tuple-element.18.refs_0_, bf16[256,2048]{1,0:T(8,128)(2,1)} %get-tuple-element.19.refs_1_, ...), custom_call_target="tpu_custom_call" | custom-call | bytes 10000000 | tf_op jit(solution)/shard_map/pallas_call | solution.py:528

commit v4 on v3

--- a/solution.py
+++ b/solution.py
@@ -285,6 +285,7 @@
         for g, (probs, ds) in enumerate(low):
             dkv[pl.ds(g * 256, 256), pl.ds(0, PW)] = dot(ds, qb[g]).astype(BF16)
             dkv[pl.ds(g * 256, 256), pl.ds(PW, PW)] = dot(probs, dob[g]).astype(BF16)
+        weight_grad(p)
         for g, (probs, ds) in enumerate(low):
             crossout[p, toks[g], :] = split(dot(probs, vp[g], TN))
             stage[2, toks[g], span] = split(dot(ds, kp[g], TN)).astype(BF16)
@@ -402,7 +403,6 @@
         def _():
             w_done(i)
             cross_pair(i)
-            weight_grad(i)
 
         @pl.when(i == PAIRS)
         def _():
@@ -441,9 +441,13 @@
 
 def finish(*refs):
     ins, outs, slabs, tail, sem = refs[:6], refs[6:12], refs[12], refs[13], refs[14]
-    held = [slabs.at[n] for n in range(5)] + [tail]
-    reads = [pltpu.make_async_copy(a, b, sem.at[0, n]) for n, (a, b) in enumerate(zip(ins, held))]
-    writes = [pltpu.make_async_copy(a, b, sem.at[1, n]) for n, (a, b) in enumerate(zip(held, outs))]
+    parts = [(ins[5], tail, outs[5])]
+    for n in range(5):
+        for piece in range(4):
+            span = pl.ds(piece * 64, 64)
+            parts.append((ins[n].at[span], slabs.at[n, span], outs[n].at[span]))
+    reads = [pltpu.make_async_copy(a, b, sem.at[0, n]) for n, (a, b, _) in enumerate(parts)]
+    writes = [pltpu.make_async_copy(b, c, sem.at[1, n]) for n, (_, b, c) in enumerate(parts)]
     for copy in reads:
         copy.start()
     for read, write in zip(reads, writes):
@@ -533,7 +537,7 @@
         scratch_shapes=[
             pltpu.VMEM((5, TOK, HEADS * HD), BF16),
             pltpu.VMEM((8, 2 * HEADS * HD), F32),
-            dma((2, 6)),
+            dma((2, 21)),
         ],
         cost_estimate=pl.CostEstimate(flops=0, bytes_accessed=10_000_000, transcendentals=0),
     )(out, dq, dk, dv, dcq, dw)

time: 82.1 us -> 84.5 us (1.029)
  Pallas kernels: 81.3 us -> 83.8 us
    pallas_call x1, Pallas kernels: 76.9 us -> 78.7 us  [on_device(): pl.pallas_call(kernel, out_shape=[slab] * 5 + [jax.ShapeDtypeStruct((8, 2...]
where the time goes in v4:
time: 84.5 us; the launch traced here: 84.4 us
  Pallas kernels  83.8 us (99%)
    pallas_call x1, Pallas kernels, on_device(): pl.pallas_call(kernel, out_shape=[slab] * 5 + [jax.ShapeDtypeStruct((8, 2...  78.7 us
    pallas_call x1, Pallas kernels, on_device(): pl.pallas_call(finish, out_shape=[slab] * 5 + [jax.ShapeDtypeStruct((8, 2...  5.06 us

profile of v4, /device:TPU:0, one launch (start us, length us, event | category | flops | bytes accessed | tf_op | source)
XLA Modules:
  0.0 84.4 jit_solution(8826076009335715612)
XLA Ops:
  0.6 78.7 %shard_map.136 = (bf16[256,2048]{1,0:T(8,128)(2,1)}, bf16[256,2048]{1,0:T(8,128)(2,1)}, bf16[256,2048]{1,0:T(8,128)(2,1)}, bf16[256,2048]{1,0:T(8,128)(2,1)}, bf...) custom-call(bf16[256,2048]{1,0:T(8,128)(2,1)} %bitcast.13, bf16[256,2048]{1,0:T(8,128)(2,1)} %bitcast.14, ...), custom_call_target="tpu_custom_call" | custom-call | flops 20000000000 | bytes 20000000 | tf_op jit(solution)/shard_map/pallas_call | solution.py:511
  79.4 5.1 %shard_map.137 = (bf16[256,2048]{1,0:T(8,128)(2,1)}, bf16[256,2048]{1,0:T(8,128)(2,1)}, bf16[256,2048]{1,0:T(8,128)(2,1)}, bf16[256,2048]{1,0:T(8,128)(2,1)}, bf...) custom-call(bf16[256,2048]{1,0:T(8,128)(2,1)} %get-tuple-element.18.refs_0_, bf16[256,2048]{1,0:T(8,128)(2,1)} %get-tuple-element.19.refs_1_, ...), custom_call_target="tpu_custom_call" | custom-call | bytes 10000000 | tf_op jit(solution)/shard_map/pallas_call | solution.py:532
